TPU v7x, 128 devices: a whole 4x4x4 slice. The times are simulated.
128 devices in a mesh: row: 8 (over z, x_hi), col: 8 (over y, core), ka: 2 (over x_lo).
Axes of the slice: x: 4 (x_hi: 2, x_lo: 2; x = x_hi * 2 + x_lo), y: 4, z: 4, core: 2. Of those that a mesh axis runs over, the one named last changes fastest.
Arguments:
- amplitudes: bfloat16 [4, 16, 1024, 1024], P(None, 'ka', 'row', 'col'), may hold values from -6 to 6
- integrals: bfloat16 [16, 1024, 4, 1024], P('ka', 'row', None, 'col'), may hold values from -0.046875 to 0.046875
Outputs:
- cycle_term: float32 [4, 4, 1024, 1024], P('ka', None, 'row', 'col')
All inputs are finite; a program needn't handle non-finite values.
Results may differ from a plain program's by a relative error of at most 0.0003.
Values may be sent and summed in bfloat16 or wider, within the bound.
A program may use at most 64 MiB of HBM per device.

v0:
```python
import jax
import jax.numpy as jnp
from jax import lax
from jax.sharding import PartitionSpec as P


def swapped(block, axis, apart):
    count = lax.axis_size(axis)
    route = []
    for low in range(count):
        high = low | 1 << apart
        if high != low and high < count:
            route += [(low, high), (high, low)]
    return lax.ppermute(block, axis, route)


def grid_hop(z_tile, hop_bit):
    return swapped(z_tile, ("row", "col"), hop_bit)


def transpose_grid(z_tile):
    grid_side = lax.axis_size("col")
    bit_count = grid_side.bit_length() - 1
    flat_index = lax.axis_index(("row", "col"))
    row_place = flat_index // grid_side
    col_place = flat_index % grid_side
    for section_bit in range(bit_count):
        first_hop = grid_hop(z_tile, section_bit)
        second_hop = grid_hop(first_hop, section_bit + bit_count)
        differ = row_place >> section_bit & 1 != col_place >> section_bit & 1
        z_tile = jnp.where(differ, second_hop, z_tile)
    return z_tile


def per_device(amplitudes, integrals):
    panel = lax.all_gather(amplitudes, "col", axis=3, tiled=True)
    partial_cycle = jnp.einsum(
        "ikac,kcjb->iajb",
        panel,
        lax.all_gather(integrals, "row", axis=1, tiled=True),
        preferred_element_type=jnp.float32,
    )
    mirrored = transpose_grid(partial_cycle)
    summed = jnp.transpose(partial_cycle, (0, 2, 1, 3)) + jnp.transpose(mirrored, (2, 0, 3, 1))
    return lax.psum_scatter(summed, "ka", scatter_dimension=0, tiled=True)


def solution(mesh):
    return jax.shard_map(
        per_device,
        mesh=mesh,
        in_specs=(P(None, "ka", "row", "col"), P("ka", "row", None, "col")),
        out_specs=P("ka", None, "row", "col"),
        check_vma=False,
    )
```

profile of v0, /device:TPU:18, one launch (start us, length us, event | category | flops | bytes accessed | tf_op | source)
XLA Modules:
  0.0 365.8 jit_solution(15293075731517556728)
XLA Ops:
  6.5 2.4 copy.6
  9.1 0.7 all-gather.3.cloned.1.call-update
  9.8 108.4 %all-gather.5.cloned.1.call-done = bf16[8,1024,4,128]{3,1,0,2:T(8,128)(2,1)} async-done(((bf16[8,128,4,128]{3,1,0,2:T(8,128)(2,1)}), bf16[8,1024,4,128]{3,1,0,2:T(8,128)(2,1)}) %all-gather.5.cloned.1.call-update) | async-done | bytes 8388624 | tf_op jit(solution)/shard_map/all_gather | solution.py:40
  118.2 54.0 %all-gather.3.cloned.1.call-done = bf16[4,8,128,1024]{3,2,1,0:T(8,128)(2,1)} async-done(((bf16[4,8,128,128]{3,2,1,0:T(8,128)(2,1)}), bf16[4,8,128,1024]{3,2,1,0:T(8,128)(2,1)}) %all-gather.3.cloned.1.call-update) | async-done | bytes 8388624 | tf_op jit(solution)/shard_map/all_gather | solution.py:36
  172.2 9.3 %fusion.3 = f32[4,128,4,128]{3,1,2,0:T(8,128)S(1)} fusion(bf16[8,1024,4,128]{3,1,0,2:T(8,128)(2,1)} %all-gather.5.cloned.1.call-done, bf16[4,8,128,1024]{3,2,1,0:T(8,128)(2,1)} %all-gather.3.cloned.1.call-done), kind=kOutput, calls=%fused_computation.3 | convolution fusion | flops 4294967296 | bytes 17825792 | tf_op jit(solution)/shard_map/ikac,kcjb->iajb/dot_general | solution.py:37
  181.6 0.3 collective-permute-start
  181.9 2.4 collective-permute-done
  184.3 2.1 collective-permute-start.1
  186.4 24.7 %collective-permute-done.1 = f32[4,128,4,128]{3,1,2,0:T(8,128)S(1)} collective-permute-done((f32[4,128,4,128]{3,1,2,0:T(8,128)S(1)}, f32[4,128,4,128]{3,1,2,0:T(8,128)S(1)}, u32[]{:S(2)}, u32[]{:S(2)}) %collective-permute-start.1) | collective-permute-done | bytes 1048608 | tf_op jit(solution)/shard_map/ppermute | solution.py:14
  211.2 0.1 broadcast_select_fusion
  211.3 0.9 collective-permute-start.2
  212.2 23.7 %collective-permute-done.2 = f32[4,128,4,128]{3,1,2,0:T(8,128)S(1)} collective-permute-done((f32[4,128,4,128]{3,1,2,0:T(8,128)S(1)}, f32[4,128,4,128]{3,1,2,0:T(8,128)S(1)}, u32[]{:S(2)}, u32[]{:S(2)}) %collective-permute-start.2) | collective-permute-done | bytes 1048608 | tf_op jit(solution)/shard_map/ppermute | solution.py:14
  235.9 1.6 collective-permute-start.3
  237.4 22.1 %collective-permute-done.3 = f32[4,128,4,128]{3,1,2,0:T(8,128)} collective-permute-done((f32[4,128,4,128]{3,1,2,0:T(8,128)S(1)}, f32[4,128,4,128]{3,1,2,0:T(8,128)}, u32[]{:S(2)}, u32[]{:S(2)}) %collective-permute-start.3) | collective-permute-done | bytes 1048608 | tf_op jit(solution)/shard_map/ppermute | solution.py:14
  259.7 0.9 collective-permute-start.4
  260.6 23.4 %collective-permute-done.4 = f32[4,128,4,128]{3,1,2,0:T(8,128)} collective-permute-done((f32[4,128,4,128]{3,1,2,0:T(8,128)S(1)}, f32[4,128,4,128]{3,1,2,0:T(8,128)}, u32[]{:S(2)}, u32[]{:S(2)}) %collective-permute-start.4) | collective-permute-done | bytes 1048608 | tf_op jit(solution)/shard_map/ppermute | solution.py:14
  284.1 3.2 collective-permute-start.5
  287.2 0.3 copy.7
  287.6 20.1 %collective-permute-done.5 = f32[4,128,4,128]{3,1,2,0:T(8,128)} collective-permute-done((f32[4,128,4,128]{3,1,2,0:T(8,128)}, f32[4,128,4,128]{3,1,2,0:T(8,128)}, u32[]{:S(2)}, u32[]{:S(2)}) %collective-permute-start.5) | collective-permute-done | bytes 1048608 | tf_op jit(solution)/shard_map/ppermute | solution.py:14
  307.6 2.4 bitcast_add_fusion
  310.1 0.6 dynamic-slice
  311.3 45.9 %all-reduce.3.cloned.1.call-done = f32[4,4,128,128]{2,3,0,1:T(8,128)} async-done(((f32[4,4,128,128]{2,3,0,1:T(8,128)}), f32[4,4,128,128]{2,3,0,1:T(8,128)}) %all-reduce.3.cloned.1.call-update) | async-done | bytes 1048592
  357.2 1.1 constant_dynamic-slice_fusion
  358.2 1.0 copy.8
  (8 shorter events, 0.2 us)
Async XLA Ops:
  6.5 111.7 %all-gather.5.cloned.1.call-start = ((), (), s32[]{:S(2)}) async-start(), calls=%async_computation.1 | async-start | bytes 9437184 | tf_op jit(solution)/shard_map/all_gather | solution.py:40
  9.0 163.2 %all-gather.3.cloned.1.call-start = ((), (), s32[]{:S(2)}) async-start(), calls=%async_computation | async-start | bytes 9437184 | tf_op jit(solution)/shard_map/all_gather | solution.py:36
  9.8 347.4 %all-reduce.3.cloned.1.call-start = ((), (), s32[]{:S(2)}) async-start(), calls=%async_computation.2 | async-start | bytes 2097152
  181.6 128.5 %copy-start = (u32[128]{0:T(128)S(1)}, u32[128]{0:T(128)}, u32[]{:S(2)}) copy-start(u32[128]{0:T(128)} %constant.42) | copy-start | bytes 1540
  181.6 2.7 collective-permute-start
  184.3 26.8 %collective-permute-start.1 = (f32[4,128,4,128]{3,1,2,0:T(8,128)S(1)}, f32[4,128,4,128]{3,1,2,0:T(8,128)S(1)}, u32[]{:S(2)}, u32[]{:S(2)}) collective-permute-start(f32[4,128,4,128]{3,1,2,0:T(8,128)S(1)} %collective-permute-done), channel_id=1, source_target_pairs={{0,16},{16,0},{2,18},{18,2},{4,20},{20,4},{6,22},{22,6},{8,24},{24... | collective-permute-start | bytes 3145736 | tf_op jit(solution)/shard_map/ppermute | solution.py:14
  211.3 24.6 %collective-permute-start.2 = (f32[4,128,4,128]{3,1,2,0:T(8,128)S(1)}, f32[4,128,4,128]{3,1,2,0:T(8,128)S(1)}, u32[]{:S(2)}, u32[]{:S(2)}) collective-permute-start(f32[4,128,4,128]{3,1,2,0:T(8,128)S(1)} %broadcast_select_fusion), channel_id=1, source_target_pairs={{0,4},{4,0},{2,6},{6,2},{8,12},{12,8},{10,14},{14,10},{16,20},{20,... | collective-permute-start | bytes 3145736 | tf_op jit(solution)/shard_map/ppermute | solution.py:14
  235.9 23.7 %collective-permute-start.3 = (f32[4,128,4,128]{3,1,2,0:T(8,128)S(1)}, f32[4,128,4,128]{3,1,2,0:T(8,128)}, u32[]{:S(2)}, u32[]{:S(2)}) collective-permute-start(f32[4,128,4,128]{3,1,2,0:T(8,128)S(1)} %collective-permute-done.2), channel_id=1, source_target_pairs={{0,32},{32,0},{2,34},{34,2},{4,36},{36,4},{6,38},{38,6},{8,40},{40... | collective-permute-start | bytes 3145736 | tf_op jit(solution)/shard_map/ppermute | solution.py:14
  259.7 24.4 %collective-permute-start.4 = (f32[4,128,4,128]{3,1,2,0:T(8,128)S(1)}, f32[4,128,4,128]{3,1,2,0:T(8,128)}, u32[]{:S(2)}, u32[]{:S(2)}) collective-permute-start(f32[4,128,4,128]{3,1,2,0:T(8,128)S(1)} %broadcast_select_fusion.1), channel_id=1, source_target_pairs={{0,8},{8,0},{2,10},{10,2},{4,12},{12,4},{6,14},{14,6},{16,24},{24,... | collective-permute-start | bytes 3145736 | tf_op jit(solution)/shard_map/ppermute | solution.py:14
  284.1 23.6 %collective-permute-start.5 = (f32[4,128,4,128]{3,1,2,0:T(8,128)}, f32[4,128,4,128]{3,1,2,0:T(8,128)}, u32[]{:S(2)}, u32[]{:S(2)}) collective-permute-start(f32[4,128,4,128]{3,1,2,0:T(8,128)} %collective-permute-done.4), channel_id=1, source_target_pairs={{0,64},{64,0},{2,66},{66,2},{4,68},{68,4},{6,70},{70,6},{8,72},{72... | collective-permute-start | bytes 3145736 | tf_op jit(solution)/shard_map/ppermute | solution.py:14
Sparse Core Ops, SparseCore 0:
  9.7 108.5 all-gather.4
  119.9 52.2 all-gather.2
  310.2 46.9 all-reduce.2
where the time goes:
time: 368 us; the launch traced here: 366 us
  waiting for transfers between devices  325 us (88%)
  between operations  13.8 us (4%)
  matrix products  9.34 us (3%)
  starting transfers between devices  9.03 us (2%)
  local copies, waits for them, and re-layouts  5.44 us (1%)
    ppermute x6, waiting for transfers between devices, swapped(): return lax.ppermute(block, axis, route)  116 us
    all_gather x1, waiting for transfers between devices, per_device(): lax.all_gather(integrals, 'row', axis=1, tiled=True)  108 us
    all_gather x1, waiting for transfers between devices, per_device(): panel = lax.all_gather(amplitudes, 'col', axis=3, tiled=True)  54 us
    unnamed x4, waiting for transfers between devices  46.6 us
    dot_general x1, matrix products, per_device(): jnp.einsum('ikac,kcjb->iajb', panel, lax.all_gather(integrals, 'row', axi...  9.34 us
    ppermute x6, starting transfers between devices, swapped(): return lax.ppermute(block, axis, route)  8.95 us
  transfers between devices with their start and end apart: 9, of which 9 were waited for; matrix products, arithmetic and copies ran while one was open for 0% of the time, Pallas kernels for 0%

commit v1 on v0

v1 whole, which is shorter than its diff:
```python
import jax
import jax.numpy as jnp
from jax import lax
from jax.experimental import pallas as pl
from jax.experimental.pallas import tpu as pltpu
from jax.sharding import PartitionSpec as P

MESH = pl.DeviceIdType.MESH
CHUNKS = 4
ROWS = 32
F32 = jnp.float32
BF16 = jnp.bfloat16


def phase_blocks(t):
    blocks = [(t, jj) for jj in range(t + 1)] + [(u, t) for u in range(t)]
    even = [b for b in blocks if b[1] % 2 == 0]
    return even, [b for b in blocks if b[1] % 2 == 1]


ORDER = [b for t in range(CHUNKS) for half in phase_blocks(t) for b in half]
PLACE = {b: e for e, b in enumerate(ORDER)}


def send(src, dst, send_sem, recv_sem, device):
    return pltpu.make_async_remote_copy(
        src_ref=src,
        dst_ref=dst,
        send_sem=send_sem,
        recv_sem=recv_sem,
        device_id=device,
        device_id_type=MESH,
    )


def arrived(ref, sem):
    pltpu.make_async_copy(ref, ref, sem).wait()


def kernel(
    a_in, b_in, out,
    a_all, b_all, b_raw, b_wide, part, sums, total, mirror,
    b_sem, a_ready, swap_send,
    an_send, an_recv, af_send, af_recv, as_send, as_recv,
    bn_send, bn_recv, bf_send, bf_recv,
    rs_send, rs_recv, t_send, t_recv,
):
    row, col, l = lax.axis_index("row"), lax.axis_index("col"), lax.axis_index("ka")
    z, h = row // 2, row % 2
    y, p = col // 2, col % 2
    x = 2 * h + l

    def dev(x, y, z, p):
        return (z * 2 + x // 2, y * 2 + p, x % 2)

    yp, ym, ya = (y + 1) % 4, (y + 3) % 4, (y + 2) % 4
    zp, zm, za = (z + 1) % 4, (z + 3) % 4, (z + 2) % 4
    y_next, y_prev = dev(x, yp, z, p), dev(x, ym, z, p)
    z_next, z_prev = dev(x, y, zp, p), dev(x, y, zm, p)
    sibling = dev(x, y, z, 1 - p)
    partner = dev((x + 2) % 4, y, z, 1 - p)
    x_others = [dev((x + d) % 4, y, z, p) for d in (1, 2, 3)]
    mirrors = [dev(2 * p + t, z, y, h) for t in (0, 1)]
    swaps = p != h
    on_self = jnp.logical_and(y == z, p == h)

    def j_of(jj):
        return ((jj % 2 + p) % 2) * 2 + jj // 2

    b_copy = pltpu.make_async_copy(b_in, b_raw, b_sem)
    b_copy.start()

    @pl.when(jnp.logical_not(swaps))
    def _():
        for u in range(CHUNKS):
            pltpu.make_async_copy(
                a_in.at[:, :, pl.ds(u * ROWS, ROWS), :], a_all.at[u, p, y], a_ready.at[u]
            ).start()

    barrier = pltpu.get_barrier_semaphore()

    def greet(device):
        pl.semaphore_signal(barrier, inc=1, device_id=device, device_id_type=MESH)

    for device in [y_next, y_prev, z_next, z_prev, sibling] + x_others:
        greet(device)

    @pl.when(swaps)
    def _():
        greet(partner)

    for t in (0, 1):
        @pl.when(jnp.logical_not(jnp.logical_and(on_self, l == t)))
        def _(t=t):
            greet(mirrors[t])

    b_copy.wait()
    for k in range(8):
        b_wide[k] = b_raw[k].astype(F32)
    for j in (0, 2, 1, 3):
        jj = (j % 2) * 2 + (j // 2 + p) % 2
        for k in range(8):
            b_all[jj, z, k] = b_wide[k, pl.ds(j, 128, stride=4), :].astype(BF16)

    peers = 9 + jnp.where(swaps, 1, 0) + jnp.where(on_self, 0, 1)
    pl.semaphore_wait(barrier, peers)

    def swap(u):
        return send(
            a_in.at[:, :, pl.ds(u * ROWS, ROWS), :],
            a_all.at[u, 1 - p, y],
            swap_send.at[u],
            a_ready.at[u],
            partner,
        )

    @pl.when(swaps)
    def _():
        for u in range(CHUNKS):
            swap(u).start()

    def a_near(u):
        slot = a_all.at[u, p, y]
        return [
            send(slot, slot, an_send.at[u, 0], an_recv.at[u, 0], y_next),
            send(slot, slot, an_send.at[u, 1], an_recv.at[u, 1], y_prev),
        ]

    def b_near(u):
        slot = b_all.at[u, z]
        return [
            send(slot, slot, bn_send.at[u, 0], bn_recv.at[u, 0], z_next),
            send(slot, slot, bn_send.at[u, 1], bn_recv.at[u, 1], z_prev),
        ]

    def a_far(u):
        one, two = a_all.at[u, p, ym, pl.ds(0, 2)], a_all.at[u, p, yp, pl.ds(2, 2)]
        return [
            send(one, one, af_send.at[u, 0], af_recv.at[u, 0], y_next),
            send(two, two, af_send.at[u, 1], af_recv.at[u, 1], y_prev),
        ]

    def b_far(u):
        one, two = b_all.at[u, zm, pl.ds(0, 4)], b_all.at[u, zp, pl.ds(4, 4)]
        return [
            send(one, one, bf_send.at[u, 0], bf_recv.at[u, 0], z_next),
            send(two, two, bf_send.at[u, 1], bf_recv.at[u, 1], z_prev),
        ]

    def a_side(u, n):
        slot = a_all.at[u, p, (y, ym, yp, ya)[n]]
        return send(slot, slot, as_send.at[u, n], as_recv.at[u, n], sibling)

    def own(u):
        arrived(a_all.at[u, p, y], a_ready.at[u])
        for copy in b_near(u) + a_near(u):
            copy.start()
        a_side(u, 0).start()

    def forward(u):
        b_copies, a_copies = b_far(u), a_far(u)
        arrived(b_all.at[u, zm], bn_recv.at[u, 0])
        b_copies[0].start()
        arrived(a_all.at[u, p, ym], an_recv.at[u, 0])
        a_copies[0].start()
        a_side(u, 1).start()
        arrived(b_all.at[u, zp], bn_recv.at[u, 1])
        b_copies[1].start()
        arrived(a_all.at[u, p, yp], an_recv.at[u, 1])
        a_copies[1].start()
        a_side(u, 2).start()

    def rs_copy(t, d):
        lo, size = t * t, 2 * t + 1
        there = (x + d) % 4
        return send(
            part.at[there // 2, pl.ds(lo, size), pl.ds((there % 2) * 2, 2)],
            sums.at[d - 1, pl.ds(lo, size)],
            rs_send.at[t, d - 1],
            rs_recv.at[t, d - 1],
            x_others[d - 1],
        )

    def multiply(t):
        arrived(a_all.at[t, p, ya, pl.ds(0, 2)], af_recv.at[t, 0])
        arrived(a_all.at[t, p, ya, pl.ds(2, 2)], af_recv.at[t, 1])
        a_side(t, 3).start()
        arrived(b_all.at[t, za, pl.ds(0, 4)], bf_recv.at[t, 0])
        arrived(b_all.at[t, za, pl.ds(4, 4)], bf_recv.at[t, 1])
        for n, place in enumerate((y, ym, yp, ya)):
            arrived(a_all.at[t, 1 - p, place], as_recv.at[t, n])
        for half in phase_blocks(t):
            for u, jj in half:
                def step(s, acc, u=u, jj=jj):
                    left = jnp.concatenate(
                        [a_all[u, :, s, :, k].reshape(8 * ROWS, 128) for k in range(8)], axis=1
                    )
                    right = b_all[jj, s].reshape(1024, 128)
                    return acc + jnp.dot(left, right, preferred_element_type=F32)

                acc = lax.fori_loop(0, 4, step, jnp.zeros((8 * ROWS, 128), F32))
                part[:, PLACE[u, jj]] = acc.reshape(2, 4, ROWS, 128)
        for d in (2, 1, 3):
            rs_copy(t, d).start()

    def span_of(t, half):
        even, odd = phase_blocks(t)
        return pl.ds(t * t + half * len(even), len(odd if half else even))

    def mirror_remote(t, half):
        span = span_of(t, half)
        there = dev(2 * p + (half + p) % 2, z, y, h)
        return send(total.at[span], mirror.at[l, span], t_send.at[t, half], t_recv.at[t, l], there)

    def mirror_local(t, half):
        span = span_of(t, half)
        return pltpu.make_async_copy(total.at[span], mirror.at[l, span], t_recv.at[t, l])

    def mirror_here(half):
        return jnp.logical_and(on_self, (half + p) % 2 == l)

    def reduce(t):
        lo, size = t * t, 2 * t + 1
        for d in (1, 3, 2):
            arrived(sums.at[d - 1, pl.ds(lo, size)], rs_recv.at[t, d - 1])
        for half in phase_blocks(t):
            for u, jj in half:
                e = PLACE[u, jj]
                value = part[h, e, pl.ds(2 * l, 2)] + sums[0, e] + sums[1, e] + sums[2, e]
                total[e] = value
                out[:, j_of(jj), pl.ds(u * ROWS, ROWS), :] = value
        for half in (0, 1):
            if phase_blocks(t)[half]:
                @pl.when(mirror_here(half))
                def _(half=half):
                    mirror_local(t, half).start()

                @pl.when(jnp.logical_not(mirror_here(half)))
                def _(half=half):
                    mirror_remote(t, half).start()

    own(0)
    own(1)
    for t in range(CHUNKS):
        forward(t)
        if t + 2 < CHUNKS:
            own(t + 2)
        if t >= 1:
            multiply(t - 1)
        if t >= 2:
            reduce(t - 2)
    multiply(CHUNKS - 1)
    reduce(CHUNKS - 2)
    reduce(CHUNKS - 1)

    for half in (0, 1):
        @pl.when((l + h) % 2 == half)
        def _(half=half):
            for t in range(CHUNKS):
                if phase_blocks(t)[half]:
                    for n in (0, 1):
                        arrived(mirror.at[n, span_of(t, half)], t_recv.at[t, n])
            for i in (0, 1):
                for n in (0, 1):
                    for m in (0, 1):
                        tile = jnp.concatenate(
                            [mirror[n, PLACE[u, 2 * i + half], m] for u in range(CHUNKS)], axis=0
                        )
                        out[i, 2 * n + m] = out[i, 2 * n + m] + tile.T

    for t in range(CHUNKS):
        for copy in a_near(t) + b_near(t) + a_far(t) + b_far(t):
            copy.wait_send()
        for n in range(4):
            a_side(t, n).wait_send()
        for d in (1, 2, 3):
            rs_copy(t, d).wait_send()
        for half in (0, 1):
            if phase_blocks(t)[half]:
                @pl.when(jnp.logical_not(mirror_here(half)))
                def _(t=t, half=half):
                    mirror_remote(t, half).wait_send()

    @pl.when(swaps)
    def _():
        for u in range(CHUNKS):
            swap(u).wait_send()


def per_device(amplitudes, integrals):
    rows = integrals.reshape(8, 512, 128)
    dma = pltpu.SemaphoreType.DMA
    n = CHUNKS
    return pl.pallas_call(
        kernel,
        out_shape=jax.ShapeDtypeStruct((2, 4, 128, 128), F32),
        in_specs=[pl.BlockSpec(memory_space=pl.ANY)] * 2,
        out_specs=pl.BlockSpec(memory_space=pltpu.VMEM),
        scratch_shapes=[
            pltpu.VMEM((n, 2, 4, 4, 8, ROWS, 128), BF16),
            pltpu.VMEM((4, 4, 8, 128, 128), BF16),
            pltpu.VMEM((8, 512, 128), BF16),
            pltpu.VMEM((8, 512, 128), F32),
            pltpu.VMEM((2, n * n, 4, ROWS, 128), F32),
            pltpu.VMEM((3, n * n, 2, ROWS, 128), F32),
            pltpu.VMEM((n * n, 2, ROWS, 128), F32),
            pltpu.VMEM((2, n * n, 2, ROWS, 128), F32),
            dma, dma((n,)), dma((n,)),
            dma((n, 2)), dma((n, 2)), dma((n, 2)), dma((n, 2)), dma((n, 4)), dma((n, 4)),
            dma((n, 2)), dma((n, 2)), dma((n, 2)), dma((n, 2)),
            dma((n, 3)), dma((n, 3)), dma((n, 2)), dma((n, 2)),
        ],
        compiler_params=pltpu.CompilerParams(
            collective_id=0, has_side_effects=True, vmem_limit_bytes=48 << 20
        ),
        cost_estimate=pl.CostEstimate(flops=4 << 30, bytes_accessed=3 << 20, transcendentals=0),
        name="cycle_contraction",
    )(amplitudes, rows)


def solution(mesh):
    return jax.shard_map(
        per_device,
        mesh=mesh,
        in_specs=(P(None, "ka", "row", "col"), P("ka", "row", None, "col")),
        out_specs=P("ka", None, "row", "col"),
        check_vma=False,
    )
```

time: 368 us -> 90.8 us (0.25)
  waiting for transfers between devices: 325 us -> 0 us
  Pallas kernels: 0 us -> 87.4 us
  between operations: 13.8 us -> 0.01 us
  matrix products: 9.34 us -> 0 us
  starting transfers between devices: 9.03 us -> 0 us
    all_gather x2 -> x0, waiting for transfers between devices: 162 us -> none  [the longest x1 108 us: per_device(): lax.all_gather(integrals, 'row', axis=1, tiled=True)]
    ppermute x6 -> x0, waiting for transfers between devices: 116 us -> none  [swapped(): return lax.ppermute(block, axis, route)]
    pallas_call x0 -> x1, Pallas kernels: none -> 87.4 us  [per_device(): pl.pallas_call(kernel, out_shape=jax.ShapeDtypeStruct((2, 4, 128, 128), F...]
    unnamed x4 -> x0, waiting for transfers between devices: 46.6 us -> none
    dot_general x1 -> x0, matrix products: 9.34 us -> none  [per_device(): jnp.einsum('ikac,kcjb->iajb', panel, lax.all_gather(integrals, 'row', axi...]
    ppermute x6 -> x0, starting transfers between devices: 8.95 us -> none  [swapped(): return lax.ppermute(block, axis, route)]
  transfers between devices with their start and end apart: 9 -> 0, of which waited for: 9 -> 0; matrix products, arithmetic and copies ran while one was open for 0% -> 0% of each run, Pallas kernels for 0% -> 0%
where the time goes in v1:
time: 90.8 us; the launch traced here: 90.6 us
  Pallas kernels  87.4 us (96%)
  local copies, waits for them, and re-layouts  3.24 us (4%)
    pallas_call x1, Pallas kernels, per_device(): pl.pallas_call(kernel, out_shape=jax.ShapeDtypeStruct((2, 4, 128, 128), F...  87.4 us
    unnamed x5, local copies, waits for them, and re-layouts  3.24 us

profile of v1, /device:TPU:18, one launch (start us, length us, event | category | flops | bytes accessed | tf_op | source)
XLA Modules:
  0.0 90.6 jit_solution(15856434261635504992)
XLA Ops:
  0.0 0.0 copy-start
  0.0 1.2 %copy-done = bf16[4,8,128,128]{3,2,1,0:T(8,128)(2,1)S(1)} copy-done((bf16[4,8,128,128]{3,2,1,0:T(8,128)(2,1)S(1)}, bf16[4,8,128,128]{3,2,1,0:T(8,128)(2,1)}, u32[]{:S(2)}) %copy-start) | copy-done | bytes 1048600
  1.2 0.0 copy-start.1
  1.2 1.2 %copy-done.1 = bf16[8,128,4,128]{3,2,1,0:T(4,128)(2,1)S(1)} copy-done((bf16[8,128,4,128]{3,2,1,0:T(4,128)(2,1)S(1)}, bf16[8,128,4,128]{3,2,1,0:T(4,128)(2,1)}, u32[]{:S(2)}) %copy-start.1) | copy-done | bytes 1048600
  2.5 87.4 %cycle_contraction.1 = f32[2,4,128,128]{3,2,1,0:T(8,128)S(1)} custom-call(bf16[4,8,128,128]{3,2,1,0:T(8,128)(2,1)S(1)} %copy-done, bf16[8,512,128]{2,1,0:T(8,128)(2,1)S(1)} %bitcast.1), custom_call_target="tpu_custom_call" | custom-call | flops 4294967296 | bytes 3145728 | tf_op jit(solution)/shard_map/cycle_contraction/pallas_call | solution.py:294
  89.8 0.8 copy.4
Async XLA Ops:
  0.0 1.2 %copy-start = (bf16[4,8,128,128]{3,2,1,0:T(8,128)(2,1)S(1)}, bf16[4,8,128,128]{3,2,1,0:T(8,128)(2,1)}, u32[]{:S(2)}) copy-start(bf16[4,8,128,128]{3,2,1,0:T(8,128)(2,1)} %a_in.1) | copy-start | bytes 3145732
  1.2 1.2 %copy-start.1 = (bf16[8,128,4,128]{3,2,1,0:T(4,128)(2,1)S(1)}, bf16[8,128,4,128]{3,2,1,0:T(4,128)(2,1)}, u32[]{:S(2)}) copy-start(bf16[8,128,4,128]{3,2,1,0:T(4,128)(2,1)} %param.3) | copy-start | bytes 3145732

commit v2 on v1

--- a/solution.py
+++ b/solution.py
@@ -12,14 +12,23 @@
 BF16 = jnp.bfloat16
 
 
-def phase_blocks(t):
-    blocks = [(t, jj) for jj in range(t + 1)] + [(u, t) for u in range(t)]
-    even = [b for b in blocks if b[1] % 2 == 0]
-    return even, [b for b in blocks if b[1] % 2 == 1]
-
-
-ORDER = [b for t in range(CHUNKS) for half in phase_blocks(t) for b in half]
-PLACE = {b: e for e, b in enumerate(ORDER)}
+GROUPS = [
+    [((t,), (jj, jj + 1)[: t + 1 - jj]) for jj in range(0, t + 1, 2)] + ([(tuple(range(t)), (t,))] if t else [])
+    for t in range(CHUNKS)
+]
+FLAT = [(t, group) for t in range(CHUNKS) for group in GROUPS[t]]
+PLACE = {}
+FIRST = []
+for _, (us, jjs) in FLAT:
+    FIRST.append(len(PLACE))
+    for jj in jjs:
+        for u in us:
+            PLACE[u, jj] = len(PLACE)
+RUNS = [
+    (g, PLACE[us[0], jj], len(us), jj % 2)
+    for g, (_, (us, jjs)) in enumerate(FLAT)
+    for jj in jjs
+]
 
 
 def send(src, dst, send_sem, recv_sem, device):
@@ -114,10 +123,13 @@
             partner,
         )
 
-    @pl.when(swaps)
-    def _():
-        for u in range(CHUNKS):
+    def start_swap(u):
+        @pl.when(swaps)
+        def _():
             swap(u).start()
+
+    start_swap(0)
+    start_swap(1)
 
     def a_near(u):
         slot = a_all.at[u, p, y]
@@ -153,6 +165,8 @@
 
     def own(u):
         arrived(a_all.at[u, p, y], a_ready.at[u])
+        if u + 2 < CHUNKS:
+            start_swap(u + 2)
         for copy in b_near(u) + a_near(u):
             copy.start()
         a_side(u, 0).start()
@@ -170,16 +184,23 @@
         a_copies[1].start()
         a_side(u, 2).start()
 
-    def rs_copy(t, d):
-        lo, size = t * t, 2 * t + 1
+    def group_size(g):
+        us, jjs = FLAT[g][1]
+        return len(us) * len(jjs)
+
+    def rs_copy(g, d):
+        span = pl.ds(FIRST[g], group_size(g))
         there = (x + d) % 4
         return send(
-            part.at[there // 2, pl.ds(lo, size), pl.ds((there % 2) * 2, 2)],
-            sums.at[d - 1, pl.ds(lo, size)],
-            rs_send.at[t, d - 1],
-            rs_recv.at[t, d - 1],
+            part.at[there // 2, span, pl.ds((there % 2) * 2, 2)],
+            sums.at[d - 1, span],
+            rs_send.at[g, d - 1],
+            rs_recv.at[g, d - 1],
             x_others[d - 1],
         )
+
+    def groups_of(t):
+        return [g for g, (when, _) in enumerate(FLAT) if when == t]
 
     def multiply(t):
         arrived(a_all.at[t, p, ya, pl.ds(0, 2)], af_recv.at[t, 0])
@@ -189,55 +210,55 @@
         arrived(b_all.at[t, za, pl.ds(4, 4)], bf_recv.at[t, 1])
         for n, place in enumerate((y, ym, yp, ya)):
             arrived(a_all.at[t, 1 - p, place], as_recv.at[t, n])
-        for half in phase_blocks(t):
-            for u, jj in half:
-                def step(s, acc, u=u, jj=jj):
+        for g in groups_of(t):
+            us, jjs = FLAT[g][1]
+            for u in us:
+                acc = None
+                for s in range(4):
                     left = jnp.concatenate(
                         [a_all[u, :, s, :, k].reshape(8 * ROWS, 128) for k in range(8)], axis=1
                     )
-                    right = b_all[jj, s].reshape(1024, 128)
-                    return acc + jnp.dot(left, right, preferred_element_type=F32)
-
-                acc = lax.fori_loop(0, 4, step, jnp.zeros((8 * ROWS, 128), F32))
-                part[:, PLACE[u, jj]] = acc.reshape(2, 4, ROWS, 128)
-        for d in (2, 1, 3):
-            rs_copy(t, d).start()
-
-    def span_of(t, half):
-        even, odd = phase_blocks(t)
-        return pl.ds(t * t + half * len(even), len(odd if half else even))
-
-    def mirror_remote(t, half):
-        span = span_of(t, half)
-        there = dev(2 * p + (half + p) % 2, z, y, h)
-        return send(total.at[span], mirror.at[l, span], t_send.at[t, half], t_recv.at[t, l], there)
-
-    def mirror_local(t, half):
-        span = span_of(t, half)
-        return pltpu.make_async_copy(total.at[span], mirror.at[l, span], t_recv.at[t, l])
-
-    def mirror_here(half):
-        return jnp.logical_and(on_self, (half + p) % 2 == l)
+                    right = jnp.concatenate([b_all[jj, s].reshape(1024, 128) for jj in jjs], axis=1)
+                    product = jnp.dot(left, right, preferred_element_type=F32)
+                    acc = product if acc is None else acc + product
+                for n, jj in enumerate(jjs):
+                    part[:, PLACE[u, jj]] = acc[:, n * 128 : (n + 1) * 128].reshape(2, 4, ROWS, 128)
+            for d in (2, 1, 3):
+                rs_copy(g, d).start()
+
+    def span_of(r):
+        return pl.ds(RUNS[r][1], RUNS[r][2])
+
+    def mirror_remote(r):
+        there = dev(2 * p + (RUNS[r][3] + p) % 2, z, y, h)
+        return send(total.at[span_of(r)], mirror.at[l, span_of(r)], t_send.at[r], t_recv.at[r, l], there)
+
+    def mirror_local(r):
+        return pltpu.make_async_copy(total.at[span_of(r)], mirror.at[l, span_of(r)], t_recv.at[r, l])
+
+    def mirror_here(r):
+        return jnp.logical_and(on_self, (RUNS[r][3] + p) % 2 == l)
 
     def reduce(t):
-        lo, size = t * t, 2 * t + 1
-        for d in (1, 3, 2):
-            arrived(sums.at[d - 1, pl.ds(lo, size)], rs_recv.at[t, d - 1])
-        for half in phase_blocks(t):
-            for u, jj in half:
-                e = PLACE[u, jj]
-                value = part[h, e, pl.ds(2 * l, 2)] + sums[0, e] + sums[1, e] + sums[2, e]
-                total[e] = value
-                out[:, j_of(jj), pl.ds(u * ROWS, ROWS), :] = value
-        for half in (0, 1):
-            if phase_blocks(t)[half]:
-                @pl.when(mirror_here(half))
-                def _(half=half):
-                    mirror_local(t, half).start()
-
-                @pl.when(jnp.logical_not(mirror_here(half)))
-                def _(half=half):
-                    mirror_remote(t, half).start()
+        for g in groups_of(t):
+            for d in (1, 3, 2):
+                arrived(sums.at[d - 1, pl.ds(FIRST[g], group_size(g))], rs_recv.at[g, d - 1])
+            us, jjs = FLAT[g][1]
+            for jj in jjs:
+                for u in us:
+                    e = PLACE[u, jj]
+                    value = part[h, e, pl.ds(2 * l, 2)] + sums[0, e] + sums[1, e] + sums[2, e]
+                    total[e] = value
+                    out[:, j_of(jj), pl.ds(u * ROWS, ROWS), :] = value
+            for r, run in enumerate(RUNS):
+                if run[0] == g:
+                    @pl.when(mirror_here(r))
+                    def _(r=r):
+                        mirror_local(r).start()
+
+                    @pl.when(jnp.logical_not(mirror_here(r)))
+                    def _(r=r):
+                        mirror_remote(r).start()
 
     own(0)
     own(1)
@@ -256,10 +277,10 @@
     for half in (0, 1):
         @pl.when((l + h) % 2 == half)
         def _(half=half):
-            for t in range(CHUNKS):
-                if phase_blocks(t)[half]:
+            for r, run in enumerate(RUNS):
+                if run[3] == half:
                     for n in (0, 1):
-                        arrived(mirror.at[n, span_of(t, half)], t_recv.at[t, n])
+                        arrived(mirror.at[n, span_of(r)], t_recv.at[r, n])
             for i in (0, 1):
                 for n in (0, 1):
                     for m in (0, 1):
@@ -273,13 +294,13 @@
             copy.wait_send()
         for n in range(4):
             a_side(t, n).wait_send()
+    for g in range(len(FLAT)):
         for d in (1, 2, 3):
-            rs_copy(t, d).wait_send()
-        for half in (0, 1):
-            if phase_blocks(t)[half]:
-                @pl.when(jnp.logical_not(mirror_here(half)))
-                def _(t=t, half=half):
-                    mirror_remote(t, half).wait_send()
+            rs_copy(g, d).wait_send()
+    for r in range(len(RUNS)):
+        @pl.when(jnp.logical_not(mirror_here(r)))
+        def _(r=r):
+            mirror_remote(r).wait_send()
 
     @pl.when(swaps)
     def _():
@@ -294,7 +315,7 @@
     return pl.pallas_call(
         kernel,
         out_shape=jax.ShapeDtypeStruct((2, 4, 128, 128), F32),
-        in_specs=[pl.BlockSpec(memory_space=pl.ANY)] * 2,
+        in_specs=[pl.BlockSpec(memory_space=pltpu.HBM)] * 2,
         out_specs=pl.BlockSpec(memory_space=pltpu.VMEM),
         scratch_shapes=[
             pltpu.VMEM((n, 2, 4, 4, 8, ROWS, 128), BF16),
@@ -308,10 +329,10 @@
             dma, dma((n,)), dma((n,)),
             dma((n, 2)), dma((n, 2)), dma((n, 2)), dma((n, 2)), dma((n, 4)), dma((n, 4)),
             dma((n, 2)), dma((n, 2)), dma((n, 2)), dma((n, 2)),
-            dma((n, 3)), dma((n, 3)), dma((n, 2)), dma((n, 2)),
+            dma((len(FLAT), 3)), dma((len(FLAT), 3)), dma((len(RUNS),)), dma((len(RUNS), 2)),
         ],
         compiler_params=pltpu.CompilerParams(
-            collective_id=0, has_side_effects=True, vmem_limit_bytes=48 << 20
+            collective_id=0, has_side_effects=True, vmem_limit_bytes=62 << 20
         ),
         cost_estimate=pl.CostEstimate(flops=4 << 30, bytes_accessed=3 << 20, transcendentals=0),
         name="cycle_contraction",

time: 90.8 us -> 82.9 us (0.913)
  Pallas kernels: 87.4 us -> 80.8 us
  local copies, waits for them, and re-layouts: 3.24 us -> 1.87 us
    pallas_call x1, Pallas kernels: 87.4 us -> 80.8 us  [per_device(): pl.pallas_call(kernel, out_shape=jax.ShapeDtypeStruct((2, 4, 128, 128), F...]
    unnamed x5 -> x1, local copies, waits for them, and re-layouts: 3.24 us -> 1.87 us
where the time goes in v2:
time: 82.9 us; the launch traced here: 82.7 us
  Pallas kernels  80.8 us (97%)
  local copies, waits for them, and re-layouts  1.87 us (2%)
    pallas_call x1, Pallas kernels, per_device(): pl.pallas_call(kernel, out_shape=jax.ShapeDtypeStruct((2, 4, 128, 128), F...  80.8 us
    unnamed x1, local copies, waits for them, and re-layouts  1.87 us

profile of v2, /device:TPU:18, one launch (start us, length us, event | category | flops | bytes accessed | tf_op | source)
XLA Modules:
  0.0 82.7 jit_solution(6298954886255617263)
XLA Ops:
  0.0 80.8 %cycle_contraction.1 = f32[2,4,128,128]{3,2,1,0:T(8,128)} custom-call(bf16[4,8,128,128]{3,2,1,0:T(8,128)(2,1)} %a_in.1, bf16[8,512,128]{2,1,0:T(8,128)(2,1)} %bitcast.1), custom_call_target="tpu_custom_call" | custom-call | flops 4294967296 | bytes 3145728 | tf_op jit(solution)/shard_map/cycle_contraction/pallas_call | solution.py:315
  80.9 1.9 %copy.4 = f32[2,4,128,128]{3,2,1,0:T(8,128)} copy(f32[2,4,128,128]{3,2,1,0:T(8,128)} %cycle_contraction.1) | data formatting | bytes 1048576

commit v3 on v2

--- a/solution.py
+++ b/solution.py
@@ -31,6 +31,29 @@
 ]
 
 
+GROUP_SIZE = [len(us) * len(jjs) for _, (us, jjs) in FLAT]
+GROUP_ROW = [64 * FIRST[g] + 16 * g for g in range(len(FLAT))]
+RUN_ROW = [64 * run[1] + 16 * r for r, run in enumerate(RUNS)]
+GROUP_ROWS = 64 * CHUNKS**2 + 16 * len(FLAT)
+RUN_ROWS = 64 * CHUNKS**2 + 16 * len(RUNS)
+
+
+def encode(values, top):
+    w = jnp.abs(values) * (255.0 / 16 / top) + 1.0 / 16
+    w2 = w * w
+    w4 = w2 * w2
+    w8 = w4 * w4
+    code = w8 * w8 * w8 * (w4 * w2 * w)
+    return jnp.where(values < 0, -code, code).astype(BF16)
+
+
+def decode(codes, top):
+    codes = codes.astype(F32)
+    w = jnp.exp2(jnp.log2(jnp.abs(codes)) * (1.0 / 31))
+    size = (w - 1.0 / 16) * (top * (16.0 / 255))
+    return jnp.where(codes < 0, -size, size)
+
+
 def send(src, dst, send_sem, recv_sem, device):
     return pltpu.make_async_remote_copy(
         src_ref=src,
@@ -48,7 +71,7 @@
 
 def kernel(
     a_in, b_in, out,
-    a_all, b_all, b_raw, b_wide, part, sums, total, mirror,
+    a_all, b_all, b_raw, b_wide, part, part16, sums16, total, total16, mirror16,
     b_sem, a_ready, swap_send,
     an_send, an_recv, af_send, af_recv, as_send, as_recv,
     bn_send, bn_recv, bf_send, bf_recv,
@@ -131,69 +154,67 @@
     start_swap(0)
     start_swap(1)
 
-    def a_near(u):
-        slot = a_all.at[u, p, y]
-        return [
-            send(slot, slot, an_send.at[u, 0], an_recv.at[u, 0], y_next),
-            send(slot, slot, an_send.at[u, 1], an_recv.at[u, 1], y_prev),
-        ]
-
-    def b_near(u):
-        slot = b_all.at[u, z]
-        return [
-            send(slot, slot, bn_send.at[u, 0], bn_recv.at[u, 0], z_next),
-            send(slot, slot, bn_send.at[u, 1], bn_recv.at[u, 1], z_prev),
-        ]
-
-    def a_far(u):
-        one, two = a_all.at[u, p, ym, pl.ds(0, 2)], a_all.at[u, p, yp, pl.ds(2, 2)]
-        return [
-            send(one, one, af_send.at[u, 0], af_recv.at[u, 0], y_next),
-            send(two, two, af_send.at[u, 1], af_recv.at[u, 1], y_prev),
-        ]
-
-    def b_far(u):
-        one, two = b_all.at[u, zm, pl.ds(0, 4)], b_all.at[u, zp, pl.ds(4, 4)]
-        return [
-            send(one, one, bf_send.at[u, 0], bf_recv.at[u, 0], z_next),
-            send(two, two, bf_send.at[u, 1], bf_recv.at[u, 1], z_prev),
-        ]
+    def a_piece(u, place, half):
+        return a_all.at[u, p, place, pl.ds(2 * half, 2)]
+
+    def b_piece(u, place, half):
+        return b_all.at[u, place, pl.ds(4 * half, 4)]
+
+    def a_near(u, way, half):
+        piece = a_piece(u, y, half)
+        return send(piece, piece, an_send.at[u, way, half], an_recv.at[u, way, half], (y_next, y_prev)[way])
+
+    def b_near(u, way, half):
+        piece = b_piece(u, z, half)
+        return send(piece, piece, bn_send.at[u, way, half], bn_recv.at[u, way, half], (z_next, z_prev)[way])
+
+    def a_far(u, way):
+        piece = a_piece(u, (ym, yp)[way], way)
+        return send(piece, piece, af_send.at[u, way], af_recv.at[u, way], (y_next, y_prev)[way])
+
+    def b_far(u, way):
+        piece = b_piece(u, (zm, zp)[way], way)
+        return send(piece, piece, bf_send.at[u, way], bf_recv.at[u, way], (z_next, z_prev)[way])
 
     def a_side(u, n):
         slot = a_all.at[u, p, (y, ym, yp, ya)[n]]
         return send(slot, slot, as_send.at[u, n], as_recv.at[u, n], sibling)
 
-    def own(u):
+    def own_first(u):
+        b_near(u, 0, 0).start()
+        b_near(u, 1, 1).start()
         arrived(a_all.at[u, p, y], a_ready.at[u])
+        a_near(u, 0, 0).start()
+        a_near(u, 1, 1).start()
+        a_side(u, 0).start()
         if u + 2 < CHUNKS:
             start_swap(u + 2)
-        for copy in b_near(u) + a_near(u):
-            copy.start()
-        a_side(u, 0).start()
-
-    def forward(u):
-        b_copies, a_copies = b_far(u), a_far(u)
-        arrived(b_all.at[u, zm], bn_recv.at[u, 0])
-        b_copies[0].start()
-        arrived(a_all.at[u, p, ym], an_recv.at[u, 0])
-        a_copies[0].start()
-        a_side(u, 1).start()
-        arrived(b_all.at[u, zp], bn_recv.at[u, 1])
-        b_copies[1].start()
-        arrived(a_all.at[u, p, yp], an_recv.at[u, 1])
-        a_copies[1].start()
-        a_side(u, 2).start()
-
-    def group_size(g):
-        us, jjs = FLAT[g][1]
-        return len(us) * len(jjs)
+
+    def own_second(u):
+        for way in (0, 1):
+            b_near(u, way, 1 - way).start()
+            a_near(u, way, 1 - way).start()
+
+    def first(u):
+        for way in (0, 1):
+            arrived(b_piece(u, (zm, zp)[way], way), bn_recv.at[u, way, way])
+            b_far(u, way).start()
+        for way in (0, 1):
+            arrived(a_piece(u, (ym, yp)[way], way), an_recv.at[u, way, way])
+            a_far(u, way).start()
+
+    def second(u):
+        for way in (0, 1):
+            arrived(b_piece(u, (zm, zp)[way], 1 - way), bn_recv.at[u, way, 1 - way])
+            arrived(a_piece(u, (ym, yp)[way], 1 - way), an_recv.at[u, way, 1 - way])
+            a_side(u, 1 + way).start()
 
     def rs_copy(g, d):
-        span = pl.ds(FIRST[g], group_size(g))
+        span = pl.ds(GROUP_ROW[g], 64 * GROUP_SIZE[g] + 16)
         there = (x + d) % 4
         return send(
-            part.at[there // 2, span, pl.ds((there % 2) * 2, 2)],
-            sums.at[d - 1, span],
+            part16.at[there // 2, there % 2, span],
+            sums16.at[d - 1, span],
             rs_send.at[g, d - 1],
             rs_recv.at[g, d - 1],
             x_others[d - 1],
@@ -212,6 +233,7 @@
             arrived(a_all.at[t, 1 - p, place], as_recv.at[t, n])
         for g in groups_of(t):
             us, jjs = FLAT[g][1]
+            top = jnp.full((1, 128), 1e-30, F32)
             for u in us:
                 acc = None
                 for s in range(4):
@@ -222,56 +244,78 @@
                     product = jnp.dot(left, right, preferred_element_type=F32)
                     acc = product if acc is None else acc + product
                 for n, jj in enumerate(jjs):
-                    part[:, PLACE[u, jj]] = acc[:, n * 128 : (n + 1) * 128].reshape(2, 4, ROWS, 128)
+                    block = acc[:, n * 128 : (n + 1) * 128]
+                    top = jnp.maximum(top, jnp.max(jnp.abs(block), axis=0, keepdims=True))
+                    part[:, PLACE[u, jj]] = block.reshape(2, 2, 2 * ROWS, 128)
+            top16 = top.astype(BF16)
+            top = top16.astype(F32)
+            for n in range(GROUP_SIZE[g]):
+                part16[:, :, pl.ds(GROUP_ROW[g] + 64 * n, 64)] = encode(part[:, FIRST[g] + n], top)
+            part16[:, :, pl.ds(GROUP_ROW[g] + 64 * GROUP_SIZE[g], 16)] = jnp.broadcast_to(top16, (2, 2, 16, 128))
             for d in (2, 1, 3):
                 rs_copy(g, d).start()
 
-    def span_of(r):
-        return pl.ds(RUNS[r][1], RUNS[r][2])
+    def run_span(r):
+        return pl.ds(RUN_ROW[r], 64 * RUNS[r][2] + 16)
 
     def mirror_remote(r):
         there = dev(2 * p + (RUNS[r][3] + p) % 2, z, y, h)
-        return send(total.at[span_of(r)], mirror.at[l, span_of(r)], t_send.at[r], t_recv.at[r, l], there)
+        return send(total16.at[run_span(r)], mirror16.at[l, run_span(r)], t_send.at[r], t_recv.at[r, l], there)
 
     def mirror_local(r):
-        return pltpu.make_async_copy(total.at[span_of(r)], mirror.at[l, span_of(r)], t_recv.at[r, l])
+        return pltpu.make_async_copy(total16.at[run_span(r)], mirror16.at[l, run_span(r)], t_recv.at[r, l])
 
     def mirror_here(r):
         return jnp.logical_and(on_self, (RUNS[r][3] + p) % 2 == l)
 
     def reduce(t):
         for g in groups_of(t):
-            for d in (1, 3, 2):
-                arrived(sums.at[d - 1, pl.ds(FIRST[g], group_size(g))], rs_recv.at[g, d - 1])
-            us, jjs = FLAT[g][1]
-            for jj in jjs:
-                for u in us:
-                    e = PLACE[u, jj]
-                    value = part[h, e, pl.ds(2 * l, 2)] + sums[0, e] + sums[1, e] + sums[2, e]
-                    total[e] = value
-                    out[:, j_of(jj), pl.ds(u * ROWS, ROWS), :] = value
-            for r, run in enumerate(RUNS):
-                if run[0] == g:
-                    @pl.when(mirror_here(r))
-                    def _(r=r):
-                        mirror_local(r).start()
-
-                    @pl.when(jnp.logical_not(mirror_here(r)))
-                    def _(r=r):
-                        mirror_remote(r).start()
-
-    own(0)
-    own(1)
+            tops = []
+            for d in (0, 2, 1):
+                arrived(sums16.at[d, pl.ds(GROUP_ROW[g], 64 * GROUP_SIZE[g] + 16)], rs_recv.at[g, d])
+            for d in range(3):
+                tops.append(sums16[d, pl.ds(GROUP_ROW[g] + 64 * GROUP_SIZE[g], 16)].astype(F32)[:1])
+            for r, (group, place, count, _) in enumerate(RUNS):
+                if group != g:
+                    continue
+                jj = FLAT[g][1][1][(place - FIRST[g]) // count]
+                top = jnp.full((1, 128), 1e-30, F32)
+                for n, u in enumerate(FLAT[g][1][0]):
+                    value = part[h, place + n, l]
+                    for d in range(3):
+                        row = GROUP_ROW[g] + 64 * (place - FIRST[g] + n)
+                        value = value + decode(sums16[d, pl.ds(row, 64)], tops[d])
+                    total[place + n] = value
+                    top = jnp.maximum(top, jnp.max(jnp.abs(value), axis=0, keepdims=True))
+                    out[:, j_of(jj), pl.ds(u * ROWS, ROWS), :] = value.reshape(2, ROWS, 128)
+                top16 = top.astype(BF16)
+                top = top16.astype(F32)
+                for n in range(count):
+                    total16[pl.ds(RUN_ROW[r] + 64 * n, 64)] = encode(total[place + n], top)
+                total16[pl.ds(RUN_ROW[r] + 64 * count, 16)] = jnp.broadcast_to(top16, (16, 128))
+
+                @pl.when(mirror_here(r))
+                def _(r=r):
+                    mirror_local(r).start()
+
+                @pl.when(jnp.logical_not(mirror_here(r)))
+                def _(r=r):
+                    mirror_remote(r).start()
+
+    own_first(0)
+    own_second(0)
     for t in range(CHUNKS):
-        forward(t)
-        if t + 2 < CHUNKS:
-            own(t + 2)
         if t >= 1:
             multiply(t - 1)
-        if t >= 2:
-            reduce(t - 2)
+        first(t)
+        if t + 1 < CHUNKS:
+            own_first(t + 1)
+        second(t)
+        if t + 1 < CHUNKS:
+            own_second(t + 1)
+        if t >= 1:
+            reduce(t - 1)
     multiply(CHUNKS - 1)
-    reduce(CHUNKS - 2)
     reduce(CHUNKS - 1)
 
     for half in (0, 1):
@@ -280,18 +324,30 @@
             for r, run in enumerate(RUNS):
                 if run[3] == half:
                     for n in (0, 1):
-                        arrived(mirror.at[n, span_of(r)], t_recv.at[r, n])
+                        arrived(mirror16.at[n, run_span(r)], t_recv.at[r, n])
+            where = {}
+            for r, (g, _, count, _) in enumerate(RUNS):
+                jj = FLAT[g][1][1][(RUNS[r][1] - FIRST[g]) // count]
+                for n, u in enumerate(FLAT[g][1][0]):
+                    where[u, jj] = RUN_ROW[r] + 64 * n, RUN_ROW[r] + 64 * count
             for i in (0, 1):
                 for n in (0, 1):
+                    pieces = []
+                    for u in range(CHUNKS):
+                        row, top_row = where[u, 2 * i + half]
+                        top = mirror16[n, pl.ds(top_row, 16)].astype(F32)[:1]
+                        pieces.append(decode(mirror16[n, pl.ds(row, 64)], top))
                     for m in (0, 1):
-                        tile = jnp.concatenate(
-                            [mirror[n, PLACE[u, 2 * i + half], m] for u in range(CHUNKS)], axis=0
-                        )
+                        tile = jnp.concatenate([piece[m * ROWS : (m + 1) * ROWS] for piece in pieces], axis=0)
                         out[i, 2 * n + m] = out[i, 2 * n + m] + tile.T
 
     for t in range(CHUNKS):
-        for copy in a_near(t) + b_near(t) + a_far(t) + b_far(t):
-            copy.wait_send()
+        for way in (0, 1):
+            for half in (0, 1):
+                a_near(t, way, half).wait_send()
+                b_near(t, way, half).wait_send()
+            a_far(t, way).wait_send()
+            b_far(t, way).wait_send()
         for n in range(4):
             a_side(t, n).wait_send()
     for g in range(len(FLAT)):
@@ -322,13 +378,15 @@
             pltpu.VMEM((4, 4, 8, 128, 128), BF16),
             pltpu.VMEM((8, 512, 128), BF16),
             pltpu.VMEM((8, 512, 128), F32),
-            pltpu.VMEM((2, n * n, 4, ROWS, 128), F32),
-            pltpu.VMEM((3, n * n, 2, ROWS, 128), F32),
-            pltpu.VMEM((n * n, 2, ROWS, 128), F32),
-            pltpu.VMEM((2, n * n, 2, ROWS, 128), F32),
+            pltpu.VMEM((2, n * n, 2, 2 * ROWS, 128), F32),
+            pltpu.VMEM((2, 2, GROUP_ROWS, 128), BF16),
+            pltpu.VMEM((3, GROUP_ROWS, 128), BF16),
+            pltpu.VMEM((n * n, 2 * ROWS, 128), F32),
+            pltpu.VMEM((RUN_ROWS, 128), BF16),
+            pltpu.VMEM((2, RUN_ROWS, 128), BF16),
             dma, dma((n,)), dma((n,)),
-            dma((n, 2)), dma((n, 2)), dma((n, 2)), dma((n, 2)), dma((n, 4)), dma((n, 4)),
-            dma((n, 2)), dma((n, 2)), dma((n, 2)), dma((n, 2)),
+            dma((n, 2, 2)), dma((n, 2, 2)), dma((n, 2)), dma((n, 2)), dma((n, 4)), dma((n, 4)),
+            dma((n, 2, 2)), dma((n, 2, 2)), dma((n, 2)), dma((n, 2)),
             dma((len(FLAT), 3)), dma((len(FLAT), 3)), dma((len(RUNS),)), dma((len(RUNS), 2)),
         ],
         compiler_params=pltpu.CompilerParams(

time: 82.9 us -> 77.5 us (0.935)
  the two profiles are of different devices: /device:TPU:18 before, /device:TPU:10 now
where the time goes in v3:
time: 77.5 us; the launch traced here: 77.4 us
  Pallas kernels  75.5 us (97%)
  local copies, waits for them, and re-layouts  1.87 us (2%)
    pallas_call x1, Pallas kernels, per_device(): pl.pallas_call(kernel, out_shape=jax.ShapeDtypeStruct((2, 4, 128, 128), F...  75.5 us
    unnamed x1, local copies, waits for them, and re-layouts  1.87 us

profile of v3, /device:TPU:10, one launch (start us, length us, event | category | flops | bytes accessed | tf_op | source)
XLA Modules:
  0.0 77.4 jit_solution(4712605072128660198)
XLA Ops:
  0.0 75.5 %cycle_contraction.1 = f32[2,4,128,128]{3,2,1,0:T(8,128)} custom-call(bf16[4,8,128,128]{3,2,1,0:T(8,128)(2,1)} %a_in.1, bf16[8,512,128]{2,1,0:T(8,128)(2,1)} %bitcast.1), custom_call_target="tpu_custom_call" | custom-call | flops 4294967296 | bytes 3145728 | tf_op jit(solution)/shard_map/cycle_contraction/pallas_call | solution.py:371
  75.5 1.9 %copy.4 = f32[2,4,128,128]{3,2,1,0:T(8,128)} copy(f32[2,4,128,128]{3,2,1,0:T(8,128)} %cycle_contraction.1) | data formatting | bytes 1048576

commit v4 on v3

v4 whole, which is shorter than its diff:
```python
import jax
import jax.numpy as jnp
from jax import lax
from jax.experimental import pallas as pl
from jax.experimental.pallas import tpu as pltpu
from jax.sharding import PartitionSpec as P

MESH = pl.DeviceIdType.MESH
CHUNKS = 4
SIZES = (32, 48, 32, 16)
STARTS = tuple(sum(SIZES[:u]) for u in range(CHUNKS))
F32 = jnp.float32
BF16 = jnp.bfloat16


GROUPS = [
    [((t,), (jj, jj + 1)[: t + 1 - jj]) for jj in range(0, t + 1, 2)] + ([(tuple(range(t)), (t,))] if t else [])
    for t in range(CHUNKS)
]
FLAT = [(t, group) for t in range(CHUNKS) for group in GROUPS[t]]
RUNS = [(g, us, jj) for g, (_, (us, jjs)) in enumerate(FLAT) for jj in jjs]


def layout(parts, pad):
    rows, spans, at = {}, [], 0
    for blocks in parts:
        first = at
        for u, jj in blocks:
            rows[u, jj] = at
            at += 2 * SIZES[u]
        spans.append((first, at - first + pad))
        at += pad
    return rows, spans, at


GROUP_BLOCKS = [[(u, jj) for jj in jjs for u in us] for _, (us, jjs) in FLAT]
RUN_BLOCKS = [[(u, jj) for u in us] for _, us, jj in RUNS]
PLAIN, _, PLAIN_ROWS = layout(GROUP_BLOCKS, 0)
GROUP_ROW, GROUP_SPAN, GROUP_ROWS = layout(GROUP_BLOCKS, 16)
RUN_ROW, RUN_SPAN, RUN_ROWS = layout(RUN_BLOCKS, 16)


def encode(values, top):
    w = jnp.abs(values) * (255.0 / 16 / top) + 1.0 / 16
    w2 = w * w
    w4 = w2 * w2
    w8 = w4 * w4
    code = w8 * w8 * w8 * (w4 * w2 * w)
    return jnp.where(values < 0, -code, code).astype(BF16)


def decode(codes, top):
    codes = codes.astype(F32)
    w = jnp.exp2(jnp.log2(jnp.abs(codes)) * (1.0 / 31))
    size = (w - 1.0 / 16) * (top * (16.0 / 255))
    return jnp.where(codes < 0, -size, size)


def send(src, dst, send_sem, recv_sem, device):
    return pltpu.make_async_remote_copy(
        src_ref=src,
        dst_ref=dst,
        send_sem=send_sem,
        recv_sem=recv_sem,
        device_id=device,
        device_id_type=MESH,
    )


def arrived(ref, sem):
    pltpu.make_async_copy(ref, ref, sem).wait()


def kernel(
    a_in, b_in, out,
    a_0, a_1, a_2, a_3, v_0, v_1, v_2, v_3, b_all, b_raw, b_wide, part, part16, sums16, total, total16, mirror16,
    b_sem, a_ready, swap_send, side_send, side_recv,
    an_send, an_recv, af_send, af_recv, as_send, as_recv,
    bn_send, bn_recv, bf_send, bf_recv,
    rs_send, rs_recv, t_send, t_recv,
):
    a_all, via = (a_0, a_1, a_2, a_3), (v_0, v_1, v_2, v_3)
    row, col, l = lax.axis_index("row"), lax.axis_index("col"), lax.axis_index("ka")
    z, h = row // 2, row % 2
    y, p = col // 2, col % 2
    x = 2 * h + l

    def dev(x, y, z, p):
        return (z * 2 + x // 2, y * 2 + p, x % 2)

    yp, ym, ya = (y + 1) % 4, (y + 3) % 4, (y + 2) % 4
    zp, zm, za = (z + 1) % 4, (z + 3) % 4, (z + 2) % 4
    y_next, y_prev = dev(x, yp, z, p), dev(x, ym, z, p)
    z_next, z_prev = dev(x, y, zp, p), dev(x, y, zm, p)
    sibling = dev(x, y, z, 1 - p)
    partner = dev((x + 2) % 4, y, z, 1 - p)
    x_others = [dev((x + d) % 4, y, z, p) for d in (1, 2, 3)]
    mirrors = [dev(2 * p + t, z, y, h) for t in (0, 1)]
    swaps = p != h
    on_self = jnp.logical_and(y == z, p == h)

    def j_of(jj):
        return ((jj % 2 + p) % 2) * 2 + jj // 2

    b_copy = pltpu.make_async_copy(b_in, b_raw, b_sem)
    b_copy.start()

    def a_part(u, half):
        return a_in.at[pl.ds(2 * half, 2), :, pl.ds(STARTS[u], SIZES[u]), :]

    @pl.when(jnp.logical_not(swaps))
    def _():
        for u in range(CHUNKS):
            for half in (0, 1):
                pltpu.make_async_copy(
                    a_part(u, half), a_all[u].at[p, y, pl.ds(2 * half, 2)], a_ready.at[u, half]
                ).start()

    barrier = pltpu.get_barrier_semaphore()

    def greet(device):
        pl.semaphore_signal(barrier, inc=1, device_id=device, device_id_type=MESH)

    for device in [y_next, y_prev, z_next, z_prev, sibling] + x_others:
        greet(device)

    @pl.when(swaps)
    def _():
        greet(partner)

    for t in (0, 1):
        @pl.when(jnp.logical_not(jnp.logical_and(on_self, l == t)))
        def _(t=t):
            greet(mirrors[t])

    def relayout(js):
        for j in js:
            jj = (j % 2) * 2 + (j // 2 + p) % 2
            for k in range(8):
                b_all[jj, z, k] = b_wide[k, pl.ds(j, 128, stride=4), :].astype(BF16)

    b_copy.wait()
    for k in range(8):
        b_wide[k] = b_raw[k].astype(F32)
    relayout((0, 2))

    peers = 9 + jnp.where(swaps, 1, 0) + jnp.where(on_self, 0, 1)
    pl.semaphore_wait(barrier, peers)

    def swap(u):
        return send(
            a_part(u, 0), a_all[u].at[1 - p, y, pl.ds(0, 2)], swap_send.at[u], a_ready.at[u, 0], partner
        )

    def swap_side(u):
        return send(a_part(u, 1), via[u], side_send.at[u], side_recv.at[u], sibling)

    def swap_on(u):
        return send(
            via[u], a_all[u].at[p, y, pl.ds(2, 2)], swap_send.at[u], a_ready.at[u, 1], x_others[1]
        )

    @pl.when(swaps)
    def _():
        for u in range(CHUNKS):
            swap_side(u).start()
            swap(u).start()

    def a_piece(u, place, half):
        return a_all[u].at[p, place, pl.ds(2 * half, 2)]

    def b_piece(u, place, half):
        return b_all.at[u, place, pl.ds(4 * half, 4)]

    def a_near(u, way, half):
        piece = a_piece(u, y, half)
        return send(piece, piece, an_send.at[u, way, half], an_recv.at[u, way, half], (y_next, y_prev)[way])

    def b_near(u, way, half):
        piece = b_piece(u, z, half)
        return send(piece, piece, bn_send.at[u, way, half], bn_recv.at[u, way, half], (z_next, z_prev)[way])

    def a_far(u, way):
        piece = a_piece(u, (ym, yp)[way], way)
        return send(piece, piece, af_send.at[u, way], af_recv.at[u, way], (y_next, y_prev)[way])

    def b_far(u, way):
        piece = b_piece(u, (zm, zp)[way], way)
        return send(piece, piece, bf_send.at[u, way], bf_recv.at[u, way], (z_next, z_prev)[way])

    def a_side(u, n):
        slot = a_all[u].at[p, (y, ym, yp, ya)[n]]
        return send(slot, slot, as_send.at[u, n], as_recv.at[u, n], sibling)

    def b_first(u):
        b_near(u, 0, 0).start()
        b_near(u, 1, 1).start()

    def b_second(u):
        b_near(u, 0, 1).start()
        b_near(u, 1, 0).start()

    def a_first(u):
        for half in (0, 1):
            arrived(a_piece(u, y, half), a_ready.at[u, half])
        a_near(u, 0, 0).start()
        a_near(u, 1, 1).start()

    def a_second(u):
        a_near(u, 0, 1).start()
        a_near(u, 1, 0).start()
        a_side(u, 0).start()

    def first(u):
        for way in (0, 1):
            arrived(b_piece(u, (zm, zp)[way], way), bn_recv.at[u, way, way])
            b_far(u, way).start()
        if u + 1 < CHUNKS:
            b_second(u + 1)
        for way in (0, 1):
            arrived(a_piece(u, (ym, yp)[way], way), an_recv.at[u, way, way])
            a_far(u, way).start()
        if u + 1 < CHUNKS:
            a_second(u + 1)

    def second(u):
        for way in (0, 1):
            arrived(b_piece(u, (zm, zp)[way], 1 - way), bn_recv.at[u, way, 1 - way])
        if u + 2 < CHUNKS:
            b_first(u + 2)
        for way in (0, 1):
            arrived(a_piece(u, (ym, yp)[way], 1 - way), an_recv.at[u, way, 1 - way])
            a_side(u, 1 + way).start()
        if u + 2 < CHUNKS:
            a_first(u + 2)

    def rs_copy(g, d):
        span = pl.ds(*GROUP_SPAN[g])
        there = (x + d) % 4
        return send(
            part16.at[there // 2, there % 2, span],
            sums16.at[d - 1, span],
            rs_send.at[g, d - 1],
            rs_recv.at[g, d - 1],
            x_others[d - 1],
        )

    def groups_of(t):
        return [g for g, (when, _) in enumerate(FLAT) if when == t]

    def product(u, jjs, places):
        total = None
        for s in places:
            left = jnp.concatenate(
                [a_all[u][:, s, :, k].reshape(8 * SIZES[u], 128) for k in range(8)], axis=1
            )
            right = jnp.concatenate([b_all[jj, s].reshape(1024, 128) for jj in jjs], axis=1)
            one = jnp.dot(left, right, preferred_element_type=F32)
            total = one if total is None else total + one
        return total

    def put(g, u, jjs, value, add):
        size = 2 * SIZES[u]
        tops = []
        for n, jj in enumerate(jjs):
            block = value[:, n * 128 : (n + 1) * 128]
            at = pl.ds(PLAIN[u, jj], size)
            if add:
                block = block + part[:, :, at].reshape(4 * size, 128)
            part[:, :, at] = block.reshape(2, 2, size, 128)
            tops.append(jnp.max(jnp.abs(block), axis=0, keepdims=True))
        return tops

    def send_group(g, tops):
        top = jnp.full((1, 128), 1e-30, F32)
        for one in tops:
            top = jnp.maximum(top, one)
        top16 = top.astype(BF16)
        top = top16.astype(F32)
        for u, jj in GROUP_BLOCKS[g]:
            size = 2 * SIZES[u]
            part16[:, :, pl.ds(GROUP_ROW[u, jj], size)] = encode(part[:, :, pl.ds(PLAIN[u, jj], size)], top)
        end = sum(GROUP_SPAN[g])
        part16[:, :, pl.ds(end - 16, 16)] = jnp.broadcast_to(top16, (2, 2, 16, 128))
        for d in (2, 1, 3):
            rs_copy(g, d).start()

    def side_arrived(t, n):
        arrived(a_all[t].at[1 - p, (y, ym, yp, ya)[n]], as_recv.at[t, n])

    def far(t):
        for way in (0, 1):
            arrived(a_piece(t, ya, way), af_recv.at[t, way])
        a_side(t, 3).start()
        for way in (0, 1):
            arrived(b_piece(t, za, way), bf_recv.at[t, way])

    def early(t):
        for n in range(3):
            side_arrived(t, n)
        for g in reversed(groups_of(t)):
            us, jjs = FLAT[g][1]
            if us == (t,) and t not in jjs:
                put(g, t, jjs, product(t, jjs, (y, ym, yp)), False)
            elif us != (t,):
                for u in us:
                    put(g, u, jjs, product(u, jjs, (z, zm, zp)), False)

    def late(t):
        far(t)
        side = True
        for g in reversed(groups_of(t)):
            us, jjs = FLAT[g][1]
            tops = []
            if us == (t,) and side:
                side_arrived(t, 3)
                side = False
            if us != (t,):
                for u in us:
                    tops += put(g, u, jjs, product(u, jjs, (za,)), True)
            else:
                if t in jjs:
                    tops += put(g, t, jjs, product(t, jjs, range(4)), False)
                else:
                    tops += put(g, t, jjs, product(t, jjs, (ya,)), True)
            send_group(g, tops)

    def run_span(r):
        return pl.ds(*RUN_SPAN[r])

    def mirror_remote(r):
        there = dev(2 * p + (RUNS[r][2] + p) % 2, z, y, h)
        return send(total16.at[run_span(r)], mirror16.at[l, run_span(r)], t_send.at[r], t_recv.at[r, l], there)

    def mirror_local(r):
        return pltpu.make_async_copy(total16.at[run_span(r)], mirror16.at[l, run_span(r)], t_recv.at[r, l])

    def mirror_here(r):
        return jnp.logical_and(on_self, (RUNS[r][2] + p) % 2 == l)

    def top_of(ref, end):
        return ref[pl.ds(end - 16, 16)].astype(F32)[:1]

    def reduce(t):
        for g in reversed(groups_of(t)):
            for d in (0, 2, 1):
                arrived(sums16.at[d, pl.ds(*GROUP_SPAN[g])], rs_recv.at[g, d])
            tops = [top_of(sums16.at[d], sum(GROUP_SPAN[g])) for d in range(3)]
            for r, (group, us, jj) in enumerate(RUNS):
                if group != g:
                    continue
                top = jnp.full((1, 128), 1e-30, F32)
                for u in us:
                    size = 2 * SIZES[u]
                    value = part[h, l, pl.ds(PLAIN[u, jj], size)]
                    for d in range(3):
                        value = value + decode(sums16[d, pl.ds(GROUP_ROW[u, jj], size)], tops[d])
                    total[pl.ds(PLAIN[u, jj], size)] = value
                    top = jnp.maximum(top, jnp.max(jnp.abs(value), axis=0, keepdims=True))
                    out[:, j_of(jj), pl.ds(STARTS[u], SIZES[u]), :] = value.reshape(2, SIZES[u], 128)
                top16 = top.astype(BF16)
                top = top16.astype(F32)
                for u in us:
                    size = 2 * SIZES[u]
                    total16[pl.ds(RUN_ROW[u, jj], size)] = encode(total[pl.ds(PLAIN[u, jj], size)], top)
                total16[pl.ds(sum(RUN_SPAN[r]) - 16, 16)] = jnp.broadcast_to(top16, (16, 128))

                @pl.when(mirror_here(r))
                def _(r=r):
                    mirror_local(r).start()

                @pl.when(jnp.logical_not(mirror_here(r)))
                def _(r=r):
                    mirror_remote(r).start()

    def sums_left(t):
        for g in groups_of(t):
            for d in (1, 2, 3):
                rs_copy(g, d).wait_send()

    def rings_left():
        for t in range(CHUNKS):
            for way in (0, 1):
                for half in (0, 1):
                    a_near(t, way, half).wait_send()
                    b_near(t, way, half).wait_send()
                a_far(t, way).wait_send()
                b_far(t, way).wait_send()
            for n in range(4):
                a_side(t, n).wait_send()

        @pl.when(swaps)
        def _():
            for u in range(CHUNKS):
                swap_side(u).wait_send()
                swap(u).wait_send()

        @pl.when(jnp.logical_not(swaps))
        def _():
            for u in range(CHUNKS):
                swap_on(u).wait_send()

    last = CHUNKS - 1
    b_first(0)
    b_second(0)
    b_first(1)

    @pl.when(jnp.logical_not(swaps))
    def _():
        a_first(0)
        a_second(0)
        a_first(1)
        for u in range(CHUNKS):
            arrived(via[u], side_recv.at[u])
            swap_on(u).start()

    relayout((1, 3))

    @pl.when(swaps)
    def _():
        a_first(0)
        a_second(0)
        a_first(1)

    for t in range(CHUNKS):
        first(t)
        second(t)
        early(t)
        if t >= 1:
            reduce(t - 1)
        late(t)
    rings_left()
    for t in range(last):
        sums_left(t)
    reduce(last)
    sums_left(last)

    for half in (0, 1):
        @pl.when((l + h) % 2 == half)
        def _(half=half):
            for r, (_, _, jj) in enumerate(RUNS):
                if jj % 2 == half:
                    for n in (0, 1):
                        arrived(mirror16.at[n, run_span(r)], t_recv.at[r, n])
            for i in (0, 1):
                jj = 2 * i + half
                for n in (0, 1):
                    pieces = []
                    for u in range(CHUNKS):
                        (r,) = [r for r, (_, us, at) in enumerate(RUNS) if u in us and at == jj]
                        top = top_of(mirror16.at[n], sum(RUN_SPAN[r]))
                        pieces.append(decode(mirror16[n, pl.ds(RUN_ROW[u, jj], 2 * SIZES[u])], top))
                    for m in (0, 1):
                        tile = jnp.concatenate(
                            [piece[m * SIZES[u] : (m + 1) * SIZES[u]] for u, piece in enumerate(pieces)], axis=0
                        )
                        out[i, 2 * n + m] = out[i, 2 * n + m] + tile.T

    for r in range(len(RUNS)):
        @pl.when(jnp.logical_not(mirror_here(r)))
        def _(r=r):
            mirror_remote(r).wait_send()


def per_device(amplitudes, integrals):
    rows = integrals.reshape(8, 512, 128)
    dma = pltpu.SemaphoreType.DMA
    n = CHUNKS
    return pl.pallas_call(
        kernel,
        out_shape=jax.ShapeDtypeStruct((2, 4, 128, 128), F32),
        in_specs=[pl.BlockSpec(memory_space=pltpu.HBM)] * 2,
        out_specs=pl.BlockSpec(memory_space=pltpu.VMEM),
        scratch_shapes=[
            *[pltpu.VMEM((2, 4, 4, 8, size, 128), BF16) for size in SIZES],
            *[pltpu.VMEM((2, 8, size, 128), BF16) for size in SIZES],
            pltpu.VMEM((4, 4, 8, 128, 128), BF16),
            pltpu.VMEM((8, 512, 128), BF16),
            pltpu.VMEM((8, 512, 128), F32),
            pltpu.VMEM((2, 2, PLAIN_ROWS, 128), F32),
            pltpu.VMEM((2, 2, GROUP_ROWS, 128), BF16),
            pltpu.VMEM((3, GROUP_ROWS, 128), BF16),
            pltpu.VMEM((PLAIN_ROWS, 128), F32),
            pltpu.VMEM((RUN_ROWS, 128), BF16),
            pltpu.VMEM((2, RUN_ROWS, 128), BF16),
            dma, dma((n, 2)), dma((n,)), dma((n,)), dma((n,)),
            dma((n, 2, 2)), dma((n, 2, 2)), dma((n, 2)), dma((n, 2)), dma((n, 4)), dma((n, 4)),
            dma((n, 2, 2)), dma((n, 2, 2)), dma((n, 2)), dma((n, 2)),
            dma((len(FLAT), 3)), dma((len(FLAT), 3)), dma((len(RUNS),)), dma((len(RUNS), 2)),
        ],
        compiler_params=pltpu.CompilerParams(
            collective_id=0, has_side_effects=True, vmem_limit_bytes=62 << 20
        ),
        cost_estimate=pl.CostEstimate(flops=4 << 30, bytes_accessed=3 << 20, transcendentals=0),
        name="cycle_contraction",
    )(amplitudes, rows)


def solution(mesh):
    return jax.shard_map(
        per_device,
        mesh=mesh,
        in_specs=(P(None, "ka", "row", "col"), P("ka", "row", None, "col")),
        out_specs=P("ka", None, "row", "col"),
        check_vma=False,
    )
```

time: 77.5 us -> 75.1 us (0.969)
  the two profiles are of different devices: /device:TPU:10 before, /device:TPU:18 now
where the time goes in v4:
time: 75.1 us; the launch traced here: 74.6 us
  Pallas kernels  72.7 us (97%)
  local copies, waits for them, and re-layouts  1.87 us (2%)
    pallas_call x1, Pallas kernels, per_device(): pl.pallas_call(kernel, out_shape=jax.ShapeDtypeStruct((2, 4, 128, 128), F...  72.7 us
    unnamed x1, local copies, waits for them, and re-layouts  1.87 us

profile of v4, /device:TPU:18, one launch (start us, length us, event | category | flops | bytes accessed | tf_op | source)
XLA Modules:
  0.0 74.6 jit_solution(12667880984399036452)
XLA Ops:
  0.0 72.7 %cycle_contraction.1 = f32[2,4,128,128]{3,2,1,0:T(8,128)} custom-call(bf16[4,8,128,128]{3,2,1,0:T(8,128)(2,1)} %a_in.1, bf16[8,512,128]{2,1,0:T(8,128)(2,1)} %bitcast.1), custom_call_target="tpu_custom_call" | custom-call | flops 4294967296 | bytes 3145728 | tf_op jit(solution)/shard_map/cycle_contraction/pallas_call | solution.py:469
  72.8 1.9 %copy.4 = f32[2,4,128,128]{3,2,1,0:T(8,128)} copy(f32[2,4,128,128]{3,2,1,0:T(8,128)} %cycle_contraction.1) | data formatting | bytes 1048576

commit v5 on v4

--- a/solution.py
+++ b/solution.py
@@ -100,7 +100,7 @@
     on_self = jnp.logical_and(y == z, p == h)
 
     def j_of(jj):
-        return ((jj % 2 + p) % 2) * 2 + jj // 2
+        return ((jj % 2 + p + y) % 2) * 2 + jj // 2
 
     b_copy = pltpu.make_async_copy(b_in, b_raw, b_sem)
     b_copy.start()
@@ -135,7 +135,7 @@
 
     def relayout(js):
         for j in js:
-            jj = (j % 2) * 2 + (j // 2 + p) % 2
+            jj = (j % 2) * 2 + (j // 2 + p + y) % 2
             for k in range(8):
                 b_all[jj, z, k] = b_wide[k, pl.ds(j, 128, stride=4), :].astype(BF16)
 
@@ -329,14 +329,14 @@
         return pl.ds(*RUN_SPAN[r])
 
     def mirror_remote(r):
-        there = dev(2 * p + (RUNS[r][2] + p) % 2, z, y, h)
+        there = dev(2 * p + (RUNS[r][2] + p + y) % 2, z, y, h)
         return send(total16.at[run_span(r)], mirror16.at[l, run_span(r)], t_send.at[r], t_recv.at[r, l], there)
 
     def mirror_local(r):
         return pltpu.make_async_copy(total16.at[run_span(r)], mirror16.at[l, run_span(r)], t_recv.at[r, l])
 
     def mirror_here(r):
-        return jnp.logical_and(on_self, (RUNS[r][2] + p) % 2 == l)
+        return jnp.logical_and(on_self, (RUNS[r][2] + p + y) % 2 == l)
 
     def top_of(ref, end):
         return ref[pl.ds(end - 16, 16)].astype(F32)[:1]
@@ -436,7 +436,7 @@
     sums_left(last)
 
     for half in (0, 1):
-        @pl.when((l + h) % 2 == half)
+        @pl.when((l + h + z) % 2 == half)
         def _(half=half):
             for r, (_, _, jj) in enumerate(RUNS):
                 if jj % 2 == half:

time: 75.1 us -> 72.4 us (0.964)
  Pallas kernels: 72.7 us -> 69.9 us
    pallas_call x1, Pallas kernels: 72.7 us -> 69.9 us  [per_device(): pl.pallas_call(kernel, out_shape=jax.ShapeDtypeStruct((2, 4, 128, 128), F...]
where the time goes in v5:
time: 72.4 us; the launch traced here: 71.8 us
  Pallas kernels  69.9 us (97%)
  local copies, waits for them, and re-layouts  1.87 us (3%)
    pallas_call x1, Pallas kernels, per_device(): pl.pallas_call(kernel, out_shape=jax.ShapeDtypeStruct((2, 4, 128, 128), F...  69.9 us
    unnamed x1, local copies, waits for them, and re-layouts  1.87 us

profile of v5, /device:TPU:18, one launch (start us, length us, event | category | flops | bytes accessed | tf_op | source)
XLA Modules:
  0.0 71.8 jit_solution(18360978305205187788)
XLA Ops:
  0.0 69.9 %cycle_contraction.1 = f32[2,4,128,128]{3,2,1,0:T(8,128)} custom-call(bf16[4,8,128,128]{3,2,1,0:T(8,128)(2,1)} %a_in.1, bf16[8,512,128]{2,1,0:T(8,128)(2,1)} %bitcast.1), custom_call_target="tpu_custom_call" | custom-call | flops 4294967296 | bytes 3145728 | tf_op jit(solution)/shard_map/cycle_contraction/pallas_call | solution.py:469
  69.9 1.9 %copy.4 = f32[2,4,128,128]{3,2,1,0:T(8,128)} copy(f32[2,4,128,128]{3,2,1,0:T(8,128)} %cycle_contraction.1) | data formatting | bytes 1048576

commit v6 on v5

--- a/solution.py
+++ b/solution.py
@@ -14,7 +14,7 @@
 
 
 GROUPS = [
-    [((t,), (jj, jj + 1)[: t + 1 - jj]) for jj in range(0, t + 1, 2)] + ([(tuple(range(t)), (t,))] if t else [])
+    [((t,), (jj, jj + 1)[: t + 1 - jj]) for jj in range(0, t + 1, 2)] + [(us, (t,)) for us in ([], [(0,)], [(0, 1)], [(2,), (1,), (0,)])[t]]
     for t in range(CHUNKS)
 ]
 FLAT = [(t, group) for t in range(CHUNKS) for group in GROUPS[t]]
@@ -141,7 +141,7 @@
 
     b_copy.wait()
     for k in range(8):
-        b_wide[k] = b_raw[k].astype(F32)
+        b_wide[k, pl.ds(0, 512)] = b_raw[k].astype(F32)
     relayout((0, 2))
 
     peers = 9 + jnp.where(swaps, 1, 0) + jnp.where(on_self, 0, 1)
@@ -435,15 +435,20 @@
     reduce(last)
     sums_left(last)
 
+    for r in range(len(RUNS)):
+        @pl.when(jnp.logical_not(mirror_here(r)))
+        def _(r=r):
+            mirror_remote(r).wait_send()
+
     for half in (0, 1):
         @pl.when((l + h + z) % 2 == half)
         def _(half=half):
-            for r, (_, _, jj) in enumerate(RUNS):
-                if jj % 2 == half:
-                    for n in (0, 1):
-                        arrived(mirror16.at[n, run_span(r)], t_recv.at[r, n])
-            for i in (0, 1):
+            for i in (1, 0):
                 jj = 2 * i + half
+                for r, run in enumerate(RUNS):
+                    if run[2] == jj:
+                        for n in (0, 1):
+                            arrived(mirror16.at[n, run_span(r)], t_recv.at[r, n])
                 for n in (0, 1):
                     pieces = []
                     for u in range(CHUNKS):
@@ -455,11 +460,6 @@
                             [piece[m * SIZES[u] : (m + 1) * SIZES[u]] for u, piece in enumerate(pieces)], axis=0
                         )
                         out[i, 2 * n + m] = out[i, 2 * n + m] + tile.T
-
-    for r in range(len(RUNS)):
-        @pl.when(jnp.logical_not(mirror_here(r)))
-        def _(r=r):
-            mirror_remote(r).wait_send()
 
 
 def per_device(amplitudes, integrals):
@@ -476,7 +476,7 @@
             *[pltpu.VMEM((2, 8, size, 128), BF16) for size in SIZES],
             pltpu.VMEM((4, 4, 8, 128, 128), BF16),
             pltpu.VMEM((8, 512, 128), BF16),
-            pltpu.VMEM((8, 512, 128), F32),
+            pltpu.VMEM((8, 520, 128), F32),
             pltpu.VMEM((2, 2, PLAIN_ROWS, 128), F32),
             pltpu.VMEM((2, 2, GROUP_ROWS, 128), BF16),
             pltpu.VMEM((3, GROUP_ROWS, 128), BF16),

time: 72.4 us -> 71.5 us (0.988)
  Pallas kernels: 69.9 us -> 68.8 us
    pallas_call x1, Pallas kernels: 69.9 us -> 68.8 us  [per_device(): pl.pallas_call(kernel, out_shape=jax.ShapeDtypeStruct((2, 4, 128, 128), F...]
where the time goes in v6:
time: 71.5 us; the launch traced here: 70.7 us
  Pallas kernels  68.8 us (96%)
  local copies, waits for them, and re-layouts  1.87 us (3%)
    pallas_call x1, Pallas kernels, per_device(): pl.pallas_call(kernel, out_shape=jax.ShapeDtypeStruct((2, 4, 128, 128), F...  68.8 us
    unnamed x1, local copies, waits for them, and re-layouts  1.87 us

profile of v6, /device:TPU:18, one launch (start us, length us, event | category | flops | bytes accessed | tf_op | source)
XLA Modules:
  0.0 70.7 jit_solution(12995113158416827527)
XLA Ops:
  0.0 68.8 %cycle_contraction.1 = f32[2,4,128,128]{3,2,1,0:T(8,128)} custom-call(bf16[4,8,128,128]{3,2,1,0:T(8,128)(2,1)} %a_in.1, bf16[8,512,128]{2,1,0:T(8,128)(2,1)} %bitcast.1), custom_call_target="tpu_custom_call" | custom-call | flops 4294967296 | bytes 3145728 | tf_op jit(solution)/shard_map/cycle_contraction/pallas_call | solution.py:469
  68.8 1.9 %copy.4 = f32[2,4,128,128]{3,2,1,0:T(8,128)} copy(f32[2,4,128,128]{3,2,1,0:T(8,128)} %cycle_contraction.1) | data formatting | bytes 1048576

commit v7 on v6

--- a/solution.py
+++ b/solution.py
@@ -189,8 +189,12 @@
         return send(piece, piece, bf_send.at[u, way], bf_recv.at[u, way], (z_next, z_prev)[way])
 
     def a_side(u, n):
-        slot = a_all[u].at[p, (y, ym, yp, ya)[n]]
+        slot = a_all[u].at[p, (y, ym, yp)[n]]
         return send(slot, slot, as_send.at[u, n], as_recv.at[u, n], sibling)
+
+    def a_side_far(u, way):
+        piece = a_piece(u, ya, way)
+        return send(piece, piece, as_send.at[u, 3 + way], as_recv.at[u, 3 + way], sibling)
 
     def b_first(u):
         b_near(u, 0, 0).start()
@@ -286,12 +290,16 @@
             rs_copy(g, d).start()
 
     def side_arrived(t, n):
-        arrived(a_all[t].at[1 - p, (y, ym, yp, ya)[n]], as_recv.at[t, n])
+        if n < 3:
+            arrived(a_all[t].at[1 - p, (y, ym, yp)[n]], as_recv.at[t, n])
+            return
+        for way in (0, 1):
+            arrived(a_all[t].at[1 - p, ya, pl.ds(2 * way, 2)], as_recv.at[t, 3 + way])
 
     def far(t):
         for way in (0, 1):
             arrived(a_piece(t, ya, way), af_recv.at[t, way])
-        a_side(t, 3).start()
+            a_side_far(t, way).start()
         for way in (0, 1):
             arrived(b_piece(t, za, way), bf_recv.at[t, way])
 
@@ -386,8 +394,10 @@
                     b_near(t, way, half).wait_send()
                 a_far(t, way).wait_send()
                 b_far(t, way).wait_send()
-            for n in range(4):
+            for n in range(3):
                 a_side(t, n).wait_send()
+            for way in (0, 1):
+                a_side_far(t, way).wait_send()
 
         @pl.when(swaps)
         def _():
@@ -484,7 +494,7 @@
             pltpu.VMEM((RUN_ROWS, 128), BF16),
             pltpu.VMEM((2, RUN_ROWS, 128), BF16),
             dma, dma((n, 2)), dma((n,)), dma((n,)), dma((n,)),
-            dma((n, 2, 2)), dma((n, 2, 2)), dma((n, 2)), dma((n, 2)), dma((n, 4)), dma((n, 4)),
+            dma((n, 2, 2)), dma((n, 2, 2)), dma((n, 2)), dma((n, 2)), dma((n, 5)), dma((n, 5)),
             dma((n, 2, 2)), dma((n, 2, 2)), dma((n, 2)), dma((n, 2)),
             dma((len(FLAT), 3)), dma((len(FLAT), 3)), dma((len(RUNS),)), dma((len(RUNS), 2)),
         ],

time: 71.5 us -> 71.6 us (level)
  no operation moved by 1% of the time
where the time goes in v7:
time: 71.6 us; the launch traced here: 71.3 us
  Pallas kernels  69.4 us (97%)
  local copies, waits for them, and re-layouts  1.87 us (3%)
    pallas_call x1, Pallas kernels, per_device(): pl.pallas_call(kernel, out_shape=jax.ShapeDtypeStruct((2, 4, 128, 128), F...  69.4 us
    unnamed x1, local copies, waits for them, and re-layouts  1.87 us

profile of v7, /device:TPU:18, one launch (start us, length us, event | category | flops | bytes accessed | tf_op | source)
XLA Modules:
  0.0 71.3 jit_solution(9727474811458016585)
XLA Ops:
  0.0 69.4 %cycle_contraction.1 = f32[2,4,128,128]{3,2,1,0:T(8,128)} custom-call(bf16[4,8,128,128]{3,2,1,0:T(8,128)(2,1)} %a_in.1, bf16[8,512,128]{2,1,0:T(8,128)(2,1)} %bitcast.1), custom_call_target="tpu_custom_call" | custom-call | flops 4294967296 | bytes 3145728 | tf_op jit(solution)/shard_map/cycle_contraction/pallas_call | solution.py:479
  69.4 1.9 %copy.4 = f32[2,4,128,128]{3,2,1,0:T(8,128)} copy(f32[2,4,128,128]{3,2,1,0:T(8,128)} %cycle_contraction.1) | data formatting | bytes 1048576
